TPU v7x, 32 devices: a whole 2x2x4 slice. The times are simulated.
32 devices in a mesh: au: 8 (over z, y), ia: 4 (over x, core).
Axes of the slice: x: 2, y: 2, z: 4, core: 2. Of those that a mesh axis runs over, the one named last changes fastest.
Arguments:
- user_emb: bfloat16 [8, 2048, 256], P('au', 'ia'), may hold values from -6 to 6
- item_emb: bfloat16 [4, 1024, 256], P('ia', 'au'), may hold values from -6 to 6
- weight: bfloat16 [256, 256], replicated, may hold values from -0.375 to 0.375
- grad_user: bfloat16 [8, 2048, 256], P('au', 'ia'), may hold values from -6 to 6
- grad_item: bfloat16 [4, 1024, 256], P('ia', 'au'), may hold values from -6 to 6
- tile_values: bfloat16 [8, 512, 128, 128], P('au', 'ia'), may hold values from 0 to 1
- tile_rows: int32 [8, 512], P('au', 'ia'), may hold values from 0 to 15
- tile_cols: int32 [8, 512], P('au', 'ia'), may hold values from 0 to 7
- tile_norm: int32 [8, 512], P('au', 'ia'), may hold values from 32 to 128
- tile_count: int32 [8, 4], P('au', 'ia'), may hold values from 64 to 128, as said below
Outputs:
- grad_user_emb: bfloat16 [8, 2048, 256], P('au', 'ia')
- grad_item_emb: bfloat16 [4, 1024, 256], P('ia', 'au')
- grad_weight: float32 [256, 256], replicated
Inputs may be any that keep to these rules, and one draw needn't show every extreme that they name: `tile_rows`: slots of one block pair may name the same tile position; their terms add. Slots at and after tile_count[a, b] are unused; some block pair has exactly 128 live slots in every draw.
All inputs are finite; a program needn't handle non-finite values.
Results may differ from a plain program's by a relative error of at most 0.025.
Values may be sent and summed in bfloat16 or wider, within the bound.
A program may use at most 64 MiB of HBM per device.

v0:
```python
import math

import jax
import jax.numpy as jnp
from jax import lax
from jax.sharding import PartitionSpec as P

slot_group = 8


def split_tiles(block, edge):
    return block.reshape(-1, edge, block.shape[-1])


def fetch_items(grad_item, edge):
    cotangent = lax.all_gather(grad_item, "au", axis=1, tiled=True)
    return (split_tiles(cotangent[0], edge), None)


def fetch_users(grad_user, edge):
    cotangent = lax.all_gather(grad_user, "ia", axis=1, tiled=True)
    return (split_tiles(cotangent[0], edge), None)


def sweep(
    tile_block,
    row_ids,
    col_ids,
    norm_ids,
    live_count,
    item_source,
    user_source,
    user_shape,
    item_shape,
):
    turn_count = (live_count + slot_group - 1) // slot_group
    placeholder = jnp.zeros((1,), jnp.float32)

    def one_turn(turn_index, totals):
        user_total, item_total = totals
        first_slot = turn_index * slot_group
        values = lax.dynamic_slice_in_dim(tile_block, first_slot, slot_group, 0)
        row_pick = lax.dynamic_slice_in_dim(row_ids, first_slot, slot_group, 0)
        col_pick = lax.dynamic_slice_in_dim(col_ids, first_slot, slot_group, 0)
        norm_pick = lax.dynamic_slice_in_dim(norm_ids, first_slot, slot_group, 0)
        live_mask = first_slot + jnp.arange(slot_group, dtype=jnp.int32) < live_count
        inverse = jnp.where(live_mask, 1.0 / norm_pick.astype(jnp.float32), 0.0)[:, None, None]
        if item_source is not None:
            forward = jnp.einsum(
                "gic,gcd->gid", values, item_source[col_pick], preferred_element_type=jnp.float32
            )
            user_total = user_total.at[row_pick].add(forward * inverse)
        if user_source is not None:
            backward = jnp.einsum(
                "gic,gid->gcd", values, user_source[row_pick], preferred_element_type=jnp.float32
            )
            item_total = item_total.at[col_pick].add(backward * inverse)
        return (user_total, item_total)

    start = (
        jnp.zeros(user_shape, jnp.float32) if item_source is not None else placeholder,
        jnp.zeros(item_shape, jnp.float32) if user_source is not None else placeholder,
    )
    return lax.fori_loop(0, turn_count, one_turn, start)


def reduce_users(user_total, width):
    return lax.psum_scatter(
        user_total.reshape(-1, width).astype(jnp.bfloat16), "ia", scatter_dimension=0, tiled=True
    ).astype(jnp.float32)


def reduce_items(item_total, width):
    return lax.psum_scatter(
        item_total.reshape(-1, width).astype(jnp.bfloat16), "au", scatter_dimension=0, tiled=True
    ).astype(jnp.float32)


def block_product(embedded, total):
    return jnp.einsum(
        "rd,re->de", embedded.astype(jnp.float32), total, precision=lax.Precision.HIGHEST
    )


def per_device(
    user_emb,
    item_emb,
    weight,
    grad_user,
    grad_item,
    tile_values,
    tile_rows,
    tile_cols,
    tile_norm,
    tile_count,
):
    width = weight.shape[0]
    edge = tile_values.shape[2]
    user_shape = (user_emb.shape[1] * lax.axis_size("ia") // edge, edge, width)
    item_shape = (item_emb.shape[1] * lax.axis_size("au") // edge, edge, width)
    tile_block = tile_values[0]
    row_ids = tile_rows[0]
    col_ids = tile_cols[0]
    norm_ids = tile_norm[0]
    live_count = tile_count[0, 0]
    item_source, item_rows = fetch_items(grad_item, edge)
    user_total, unused = sweep(
        tile_block,
        row_ids,
        col_ids,
        norm_ids,
        live_count,
        item_source,
        None,
        user_shape,
        item_shape,
    )
    q_user = reduce_users(user_total, width)
    user_source, user_rows = fetch_users(grad_user, edge)
    unused, item_total = sweep(
        tile_block,
        row_ids,
        col_ids,
        norm_ids,
        live_count,
        None,
        user_source,
        user_shape,
        item_shape,
    )
    q_item = reduce_items(item_total, width)
    weight_part = block_product(user_emb[0], q_user) + block_product(item_emb[0], q_item)
    user_count = user_emb.shape[1] * lax.axis_size("ia") * lax.axis_size("au")
    item_count = item_emb.shape[1] * lax.axis_size("au") * lax.axis_size("ia")
    grad_weight = lax.psum(weight_part, ("au", "ia")) / math.sqrt(user_count + item_count)
    grad_user_emb = jnp.einsum(
        "re,de->rd", q_user.astype(jnp.bfloat16), weight, preferred_element_type=jnp.float32
    ).astype(jnp.bfloat16)
    grad_item_emb = jnp.einsum(
        "re,de->rd", q_item.astype(jnp.bfloat16), weight, preferred_element_type=jnp.float32
    ).astype(jnp.bfloat16)
    return (grad_user_emb[None], grad_item_emb[None], grad_weight)


def solution(mesh):
    return jax.shard_map(
        per_device,
        mesh=mesh,
        in_specs=(
            P("au", "ia", None),
            P("ia", "au", None),
            P(),
            P("au", "ia", None),
            P("ia", "au", None),
            P("au", "ia", None, None),
            P("au", "ia"),
            P("au", "ia"),
            P("au", "ia"),
            P("au", "ia"),
        ),
        out_specs=(P("au", "ia", None), P("ia", "au", None), P()),
        check_vma=False,
    )
```

profile of v0, /device:TPU:0, one launch (start us, length us, event | category | flops | bytes accessed | tf_op | source)
XLA Modules:
  0.0 430.0 jit_solution(6445473050450955679)
XLA Ops:
  8.7 33.3 %all_gather.6 = bf16[1,1024,256]{2,1,0:T(8,128)(2,1)S(1)} all-gather(bf16[1,128,256]{2,1,0:T(8,128)(2,1)} %param.18), channel_id=1, replica_groups=mesh['au'=8,'ia'=4] {'au'}, dimensions={1}, use_global_device_ids=true | all-gather | bytes 589824 | tf_op jit(solution)/shard_map/all_gather | solution.py:16
  43.5 71.0 %while.20 = (s32[]{:T(128)}, f32[16,128,256]{2,1,0:T(8,128)}, s32[]{:T(128)}, s32[128]{0:T(128)S(1)}, bf16[128,128,128]{2,1,0:T(8,128)(2,1)}, /*index=5*/s32[128...) while((s32[]{:T(128)}, f32[16,128,256]{2,1,0:T(8,128)}, ...), condition=%wide.region_2.3_spmd, body=%wide.region_0.2_spmd.sunk | while | flops 67634272 | bytes 6033919 | solution.py:64
  46.2 3.2 scatter_fusion
  52.0 3.2 scatter_fusion
  57.9 3.3 scatter_fusion
  63.8 3.3 scatter_fusion
  69.8 3.3 scatter_fusion
  75.8 3.3 scatter_fusion
  81.6 3.3 scatter_fusion
  87.6 3.3 scatter_fusion
  93.5 3.3 scatter_fusion
  99.4 3.3 scatter_fusion
  105.3 3.3 scatter_fusion
  111.2 3.3 scatter_fusion
  114.5 2.7 convert_element_type.30
  117.3 6.4 %copy.13 = bf16[1,128,128,128]{2,3,1,0:T(8,128)(2,1)} copy(bf16[1,128,128,128]{3,2,1,0:T(8,128)(2,1)} %bitcast.37) | data formatting | bytes 8388608 | tf_op args[5]
  123.7 62.8 %while.21 = (s32[]{:T(128)}, f32[8,128,256]{2,1,0:T(8,128)S(1)}, s32[]{:T(128)}, s32[128]{0:T(128)S(1)}, bf16[128,128,128]{1,2,0:T(8,128)(2,1)}, /*index=5*/s32[...) while((s32[]{:T(128)}, f32[8,128,256]{2,1,0:T(8,128)S(1)}, ...), condition=%wide.region_6.7_spmd, body=%wide.region_4.6_spmd.sunk | while | flops 67634272 | bytes 6033919 | solution.py:64
  124.6 1.8 gather_fusion.1
  129.8 1.8 gather_fusion.1
  135.0 1.8 gather_fusion.1
  140.2 1.8 gather_fusion.1
  145.5 1.9 gather_fusion.1
  150.8 1.8 gather_fusion.1
  156.0 1.8 gather_fusion.1
  161.2 1.8 gather_fusion.1
  166.5 1.8 gather_fusion.1
  171.7 1.8 gather_fusion.1
  176.9 1.8 gather_fusion.1
  182.2 1.8 gather_fusion.1
  188.8 102.8 %reduce-scatter.5.cloned.1.call-done = bf16[128,256]{1,0:T(8,128)(2,1)} async-done(((bf16[1024,256]{1,0:T(8,128)(2,1)}), bf16[128,256]{1,0:T(8,128)(2,1)}) %reduce-scatter.5.cloned.1.call-update) | async-done | bytes 65552 | tf_op jit(solution)/shard_map/reduce_scatter | solution.py:74
  293.3 1.9 fusion.4
  296.9 124.8 %all-reduce.2.cloned.1.call-done = f32[256,256]{0,1:T(8,128)} async-done(((f32[256,256]{0,1:T(8,128)}), f32[256,256]{0,1:T(8,128)}) %all-reduce.2.cloned.1.call-update) | async-done | bytes 262160 | tf_op jit(solution)/shard_map/psum | solution.py:135
  (150 shorter events, 81.9 us)
Async XLA Ops:
  7.2 180.4 %copy-start = (bf16[1,512,256]{2,1,0:T(8,128)(2,1)S(1)}, bf16[1,512,256]{2,1,0:T(8,128)(2,1)}, u32[]{:S(2)}) copy-start(bf16[1,512,256]{2,1,0:T(8,128)(2,1)} %param.14) | copy-start | bytes 786436
  7.2 36.3 %copy-start.3 = (s32[1,128]{1,0:T(1,128)S(1)}, s32[1,128]{1,0:T(1,128)}, u32[]{:S(2)}) copy-start(s32[1,128]{1,0:T(1,128)} %param.20) | copy-start | bytes 1540
  7.2 36.3 %copy-start.4 = (s32[1,128]{1,0:T(1,128)S(1)}, s32[1,128]{1,0:T(1,128)}, u32[]{:S(2)}) copy-start(s32[1,128]{1,0:T(1,128)} %param.21) | copy-start | bytes 1540
  7.2 36.3 %copy-start.5 = (s32[1,128]{1,0:T(1,128)S(1)}, s32[1,128]{1,0:T(1,128)}, u32[]{:S(2)}) copy-start(s32[1,128]{1,0:T(1,128)} %param.22) | copy-start | bytes 1540
  7.2 116.4 %all-gather.2.cloned.1.call-start = ((), (), s32[]{:S(2)}) async-start(), calls=%async_computation.3 | async-start | bytes 1310720 | tf_op jit(solution)/shard_map/all_gather | solution.py:21
  7.9 179.6 %reduce-scatter.3.cloned.1.call-start = ((), (), s32[]{:S(2)}) async-start(), calls=%async_computation.2 | async-start | bytes 1310720 | tf_op jit(solution)/shard_map/reduce_scatter | solution.py:68
  117.2 174.3 %reduce-scatter.5.cloned.1.call-start = ((), (), s32[]{:S(2)}) async-start(), calls=%async_computation.4 | async-start | bytes 589824 | tf_op jit(solution)/shard_map/reduce_scatter | solution.py:74
  186.6 105.0 %copy-start.2 = (bf16[1,128,256]{2,1,0:T(8,128)(2,1)S(1)}, bf16[1,128,256]{2,1,0:T(8,128)(2,1)}, u32[]{:S(2)}) copy-start(bf16[1,128,256]{2,1,0:T(8,128)(2,1)} %param.15) | copy-start | bytes 196612
  186.6 106.8 %copy-start.1 = (bf16[256,256]{1,0:T(8,128)(2,1)S(1)}, bf16[256,256]{1,0:T(8,128)(2,1)}, u32[]{:S(2)}) copy-start(bf16[256,256]{1,0:T(8,128)(2,1)} %param.16) | copy-start | bytes 393220
  187.5 234.2 %all-reduce.2.cloned.1.call-start = ((), (), s32[]{:S(2)}) async-start(), calls=%async_computation.5 | async-start | bytes 524288 | tf_op jit(solution)/shard_map/psum | solution.py:135
Sparse Core Ops, SparseCore 0:
  9.6 19.4 all-gather.1
  117.3 45.9 reduce-scatter.2
  187.6 103.9 reduce-scatter.4
  297.5 124.1 all-reduce.1
where the time goes:
time: 432 us; the launch traced here: 430 us
  waiting for transfers between devices  228 us (53%)
  other arithmetic  79 us (18%)
  local copies, waits for them, and re-layouts  37.7 us (9%)
  matrix products  36.2 us (8%)
  blocking collectives  33.3 us (8%)
  between operations  14.5 us (3%)
    psum x1, waiting for transfers between devices, per_device(): lax.psum(weight_part, ('au', 'ia')) / math.sqrt(user_count + item_count)  125 us
    reduce_scatter x1, waiting for transfers between devices, reduce_items(): lax.psum_scatter(item_total.reshape(-1, width).astype(jnp.bfloat16), 'au'...  103 us
    scatter-add x12, other arithmetic, one_turn(): user_total = user_total.at[row_pick].add(forward * inverse)  39.2 us
    all_gather x1, blocking collectives, fetch_items(): cotangent = lax.all_gather(grad_item, 'au', axis=1, tiled=True)  33.3 us
    gather x12, local copies, waits for them, and re-layouts, one_turn(): user_source[row_pick]  21.8 us
    select_n x24, other arithmetic, one_turn(): jnp.where(live_mask, 1.0 / norm_pick.astype(jnp.float32), 0.0)  17.4 us
    scatter-add x12, other arithmetic, one_turn(): item_total = item_total.at[col_pick].add(backward * inverse)  15.9 us
    dot_general x12, matrix products, one_turn(): jnp.einsum('gic,gid->gcd', values, user_source[row_pick], preferred_eleme...  14.9 us
  transfers between devices with their start and end apart: 4, of which 2 were waited for; matrix products, arithmetic and copies ran while one was open for 35% of the time, Pallas kernels for 0%

commit v1 on v0

v1 whole, which is shorter than its diff:
```python
import functools
import math

import jax
import jax.numpy as jnp
from jax import lax
from jax.experimental import pallas as pl
from jax.experimental.pallas import tpu as pltpu
from jax.sharding import PartitionSpec as P

MESH = pl.DeviceIdType.MESH
LOAD_PARTS = 8
LANES = 128


def remote(src, dst, send_sem, recv_sem, target):
    return pltpu.make_async_remote_copy(
        src_ref=src,
        dst_ref=dst,
        send_sem=send_sem,
        recv_sem=recv_sem,
        device_id=target,
        device_id_type=MESH,
    )


def block_of(ref, index, rows):
    return ref.at[pl.ds(pl.multiple_of(index * rows, rows), rows)]


def take(ref, index, rows):
    return ref[pl.ds(pl.multiple_of(index * rows, rows), rows), :]


class Ring:
    def __init__(self, axis, size):
        self.axis = axis
        self.half = size // 2
        self.me = lax.axis_index(axis)
        self.pair = self.me // 2
        self.side = self.me % 2

    def ahead(self, step):
        return (self.pair + step) % self.half

    def behind(self, step):
        return (self.pair + self.half - step) % self.half

    def same(self, pair):
        return 2 * pair + self.side

    def other(self, pair):
        return 2 * pair + 1 - self.side

    def at(self, index):
        return {self.axis: index}


class Gather:
    def __init__(self, ring, shard, full, sems):
        self.ring, self.shard, self.full = ring, shard, full
        self.rows = shard.shape[0]
        self.near_send, self.near_recv, self.far_send, self.far_recv = sems

    def near(self, step, arriving=False):
        ring = self.ring
        target = ring.other(ring.pair) if step == 0 else ring.same(ring.ahead(step))
        origin = ring.other(ring.pair) if step == 0 else ring.same(ring.behind(step))
        block = block_of(self.full, origin if arriving else ring.me, self.rows)
        return remote(
            self.shard, block, self.near_send.at[step], self.near_recv.at[step], ring.at(target)
        )

    def far(self, step, arriving=False):
        ring = self.ring
        behind = ring.behind(step)
        source = block_of(self.full, ring.same(behind), self.rows)
        landing = block_of(self.full, ring.other(behind), self.rows) if arriving else source
        return remote(
            source,
            landing,
            self.far_send.at[step],
            self.far_recv.at[step],
            ring.at(ring.other(ring.pair)),
        )

    def start(self):
        for step in range(1, self.ring.half):
            self.near(step).start()
        self.near(0).start()

    def keep_own(self):
        self.full[pl.ds(pl.multiple_of(self.ring.me * self.rows, self.rows), self.rows), :] = (
            self.shard[...]
        )

    def forward(self, step):
        self.near(step, True).wait_recv()
        self.far(step).start()

    def finish(self):
        self.near(0, True).wait_recv()
        for step in range(1, self.ring.half):
            self.far(step, True).wait_recv()

    def drain(self):
        for step in range(self.ring.half):
            self.near(step).wait_send()
        for step in range(1, self.ring.half):
            self.far(step).wait_send()


class Reduce:
    def __init__(self, ring, terms, near_land, far_out, far_land, sems):
        self.ring, self.terms = ring, terms
        self.near_land, self.far_out, self.far_land = near_land, far_out, far_land
        self.rows = near_land.shape[1]
        self.near_send, self.near_recv, self.far_send, self.far_recv = sems

    def near(self, step):
        ring = self.ring
        return remote(
            block_of(self.terms, ring.other(ring.ahead(step)), self.rows),
            self.near_land.at[step],
            self.near_send.at[step],
            self.near_recv.at[step],
            ring.at(ring.other(ring.pair)),
        )

    def far(self, step):
        ring = self.ring
        return remote(
            self.far_out.at[step],
            self.far_land.at[step],
            self.far_send.at[step],
            self.far_recv.at[step],
            ring.at(ring.same(ring.ahead(step))),
        )

    def order(self):
        return [*range(1, self.ring.half), 0]

    def start(self):
        for step in self.order():
            self.near(step).start()

    def joined(self, step):
        self.near(step).wait_recv()
        mine = take(self.terms, self.ring.same(self.ring.ahead(step)), self.rows)
        return mine.astype(jnp.float32) + self.near_land[step].astype(jnp.float32)

    def pass_on(self):
        for step in range(1, self.ring.half):
            self.far_out[step] = self.joined(step).astype(jnp.bfloat16)
            self.far(step).start()

    def finish(self):
        total = self.joined(0)
        for step in range(1, self.ring.half):
            self.far(step).wait_recv()
            total = total + self.far_land[step].astype(jnp.float32)
        return total

    def drain(self):
        for step in range(self.ring.half):
            self.near(step).wait_send()
        for step in range(1, self.ring.half):
            self.far(step).wait_send()


def dot(left, right, dims):
    return lax.dot_general(left, right, (dims, ((), ())), preferred_element_type=jnp.float32)


def embedded_product(embedded, total, low):
    rest = (total - low.astype(jnp.float32)).astype(jnp.bfloat16)
    return dot(embedded, low, ((0,), (0,))) + dot(embedded, rest, ((0,), (0,)))


def kernel(
    sizes,
    link_ref,
    scale_ref,
    user_emb,
    item_emb,
    weight,
    grad_user,
    grad_item,
    tiles_hbm,
    out_user,
    out_item,
    out_weight,
    tiles,
    sums,
    adjacency,
    user_full,
    item_full,
    user_terms,
    item_terms,
    user_near,
    user_out,
    user_far,
    item_near,
    item_out,
    item_far,
    piece_out,
    piece_land,
    piece_own,
    piece_all,
    load_sem,
    ia_gather_sems,
    au_gather_sems,
    ia_reduce_sems,
    au_reduce_sems,
    piece_sems,
):
    n_au, n_ia, in_kernel, factor = sizes
    count = n_au * n_ia
    cap, edge = tiles.shape[0], tiles.shape[1]
    users, items = adjacency.shape
    user_tiles, item_tiles = users // edge, items // edge
    au, ia = Ring("au", n_au), Ring("ia", n_ia)
    me = au.me * n_ia + ia.me

    def peer(index):
        return (index // n_ia, index % n_ia)

    part = cap // LOAD_PARTS

    def load(index):
        span = pl.ds(index * part, part)
        return pltpu.make_async_copy(tiles_hbm.at[span], tiles.at[span], load_sem.at[index])

    for index in range(LOAD_PARTS):
        load(index).start()

    barrier = pltpu.get_barrier_semaphore()
    if in_kernel:

        def greet(step, carry):
            pl.semaphore_signal(
                barrier, inc=1, device_id=peer((me + step) % count), device_id_type=MESH
            )
            return carry

        lax.fori_loop(1, count, greet, 0)
        pl.semaphore_wait(barrier, count - 1)
    else:
        for ring in (au, ia):
            pl.semaphore_signal(
                barrier, inc=1, device_id=ring.at(ring.other(ring.pair)), device_id_type=MESH
            )
            for step in range(1, ring.half):
                pl.semaphore_signal(
                    barrier,
                    inc=1,
                    device_id=ring.at(ring.same(ring.ahead(step))),
                    device_id_type=MESH,
                )
        pl.semaphore_wait(barrier, au.half + ia.half)

    gather_user = Gather(ia, grad_user, user_full, [ia_gather_sems.at[i] for i in range(4)])
    gather_item = Gather(au, grad_item, item_full, [au_gather_sems.at[i] for i in range(4)])
    gather_item.start()
    gather_user.start()
    gather_user.keep_own()
    gather_item.keep_own()

    sums[0] = jnp.zeros(sums.shape[1:], jnp.float32)

    def add_slot(slot, carry):
        sums[slot + 1] = (
            tiles[slot].astype(jnp.float32) * scale_ref[slot] + sums[link_ref[slot]]
        )
        return carry

    for index in range(LOAD_PARTS):
        load(index).wait()
        lax.fori_loop(index * part, (index + 1) * part, add_slot, 0)

    for step in range(1, min(au.half, 2)):
        gather_item.forward(step)

    def place_row(row, carry):
        for column in range(item_tiles):
            tile = sums[link_ref[cap + row * item_tiles + column]]
            adjacency[
                pl.ds(pl.multiple_of(row * edge, edge), edge), pl.ds(column * edge, edge)
            ] = tile.astype(jnp.bfloat16)
        return carry

    lax.fori_loop(0, user_tiles, place_row, 0)

    for step in range(2, au.half):
        gather_item.forward(step)
    for step in range(1, ia.half):
        gather_user.forward(step)

    wide = 2 * edge
    gather_user.finish()

    def item_product(index, carry):
        start = pl.multiple_of(index * wide, wide)
        product = dot(adjacency[:, pl.ds(start, wide)], user_full[...], ((0,), (0,)))
        item_terms[pl.ds(start, wide), :] = product.astype(jnp.bfloat16)
        return carry

    lax.fori_loop(0, items // wide, item_product, 0)
    reduce_item = Reduce(
        au, item_terms, item_near, item_out, item_far, [au_reduce_sems.at[i] for i in range(4)]
    )
    reduce_item.start()

    gather_item.finish()

    def user_product(index, carry):
        start = pl.multiple_of(index * wide, wide)
        product = dot(adjacency[pl.ds(start, wide), :], item_full[...], ((1,), (0,)))
        user_terms[pl.ds(start, wide), :] = product.astype(jnp.bfloat16)
        return carry

    lax.fori_loop(0, users // wide, user_product, 0)
    reduce_user = Reduce(
        ia, user_terms, user_near, user_out, user_far, [ia_reduce_sems.at[i] for i in range(4)]
    )
    reduce_user.start()
    reduce_user.pass_on()
    reduce_item.pass_on()

    q_user = reduce_user.finish()
    user_low = q_user.astype(jnp.bfloat16)
    out_user[...] = dot(user_low, weight[...], ((1,), (1,))).astype(jnp.bfloat16)
    term = embedded_product(user_emb[...], q_user, user_low)
    q_item = reduce_item.finish()
    item_low = q_item.astype(jnp.bfloat16)
    term = term + embedded_product(item_emb[...], q_item, item_low)

    if in_kernel:
        piece_rows = piece_out.shape[1]
        columns = out_weight.shape[1] // LANES
        for index in range(count):
            row, column = index // columns, index % columns
            piece_out[index] = term[
                row * piece_rows : (row + 1) * piece_rows, column * LANES : (column + 1) * LANES
            ].astype(jnp.bfloat16)

        def scatter(step):
            target = (me + step) % count
            return remote(
                piece_out.at[target],
                piece_land.at[step],
                piece_sems.at[0, step],
                piece_sems.at[1, step],
                peer(target),
            )

        def spread(step, arriving=False):
            origin = (me + count - step) % count
            return remote(
                piece_own,
                piece_all.at[origin if arriving else me],
                piece_sems.at[2, step],
                piece_sems.at[3, step],
                peer((me + step) % count),
            )

        def run(action):
            def body(step, carry):
                action(step)
                return carry

            lax.fori_loop(1, count, body, 0)

        run(lambda step: scatter(step).start())
        out_item[...] = dot(item_low, weight[...], ((1,), (1,))).astype(jnp.bfloat16)
        run(lambda step: scatter(step).wait_recv())
        total = piece_out[me].astype(jnp.float32)
        for step in range(1, count):
            total = total + piece_land[step].astype(jnp.float32)
        piece_own[...] = total.astype(jnp.bfloat16)
        run(lambda step: spread(step).start())
        piece_all[me] = piece_own[...]
        run(lambda step: spread(step, True).wait_recv())
        for index in range(count):
            row, column = index // columns, index % columns
            out_weight[
                row * piece_rows : (row + 1) * piece_rows, column * LANES : (column + 1) * LANES
            ] = (piece_all[index].astype(jnp.float32) * factor)
        run(lambda step: scatter(step).wait_send())
        run(lambda step: spread(step).wait_send())
    else:
        out_item[...] = dot(item_low, weight[...], ((1,), (1,))).astype(jnp.bfloat16)
        out_weight[...] = term * factor

    gather_user.drain()
    gather_item.drain()
    reduce_user.drain()
    reduce_item.drain()


def per_device(
    user_emb,
    item_emb,
    weight,
    grad_user,
    grad_item,
    tile_values,
    tile_rows,
    tile_cols,
    tile_norm,
    tile_count,
):
    n_au, n_ia = lax.axis_size("au"), lax.axis_size("ia")
    count = n_au * n_ia
    width = weight.shape[0]
    cap, edge = tile_values.shape[1:3]
    user_rows, item_rows = user_emb.shape[1], item_emb.shape[1]
    users, items = user_rows * n_ia, item_rows * n_au
    item_tiles = items // edge
    places = (users // edge) * item_tiles

    slots = jnp.arange(cap, dtype=jnp.int32)
    live = slots < tile_count[0, 0]
    place = jnp.where(live, tile_rows[0] * item_tiles + tile_cols[0], -1)
    wanted = jnp.concatenate([place, jnp.arange(places, dtype=jnp.int32)])
    limit = jnp.concatenate([slots, jnp.full((places,), cap, jnp.int32)])
    match = (place[None] == wanted[:, None]) & (slots[None] < limit[:, None])
    links = jnp.max(jnp.where(match, slots[None] + 1, 0), axis=1)
    scale = jnp.where(live, 1.0 / tile_norm[0].astype(jnp.float32), 0.0)

    piece_rows = width * (width // LANES) // count
    in_kernel = piece_rows % 16 == 0 and piece_rows > 0 and width % piece_rows == 0
    pieces = count if in_kernel else 1
    piece_rows = piece_rows if in_kernel else 16
    factor = 1.0 / math.sqrt(users * n_au + items * n_ia)
    half_au, half_ia = n_au // 2, n_ia // 2
    bf16, f32 = jnp.bfloat16, jnp.float32
    vmem = pl.BlockSpec(memory_space=pltpu.VMEM)
    smem = pl.BlockSpec(memory_space=pltpu.SMEM)
    dma = pltpu.SemaphoreType.DMA

    outs = pl.pallas_call(
        functools.partial(kernel, (n_au, n_ia, in_kernel, factor)),
        out_shape=(
            jax.ShapeDtypeStruct((user_rows, width), bf16),
            jax.ShapeDtypeStruct((item_rows, width), bf16),
            jax.ShapeDtypeStruct((width, width), f32),
        ),
        in_specs=[smem, smem, vmem, vmem, vmem, vmem, vmem, pl.BlockSpec(memory_space=pl.ANY)],
        out_specs=(vmem, vmem, vmem),
        scratch_shapes=[
            pltpu.VMEM((cap, edge, edge), bf16),
            pltpu.VMEM((cap + 1, edge, edge), f32),
            pltpu.VMEM((users, items), bf16),
            pltpu.VMEM((users, width), bf16),
            pltpu.VMEM((items, width), bf16),
            pltpu.VMEM((users, width), bf16),
            pltpu.VMEM((items, width), bf16),
            pltpu.VMEM((half_ia, user_rows, width), bf16),
            pltpu.VMEM((half_ia, user_rows, width), bf16),
            pltpu.VMEM((half_ia, user_rows, width), bf16),
            pltpu.VMEM((half_au, item_rows, width), bf16),
            pltpu.VMEM((half_au, item_rows, width), bf16),
            pltpu.VMEM((half_au, item_rows, width), bf16),
            pltpu.VMEM((pieces, piece_rows, LANES), bf16),
            pltpu.VMEM((pieces, piece_rows, LANES), bf16),
            pltpu.VMEM((piece_rows, LANES), bf16),
            pltpu.VMEM((pieces, piece_rows, LANES), bf16),
            dma((LOAD_PARTS,)),
            dma((4, half_ia)),
            dma((4, half_au)),
            dma((4, half_ia)),
            dma((4, half_au)),
            dma((4, pieces)),
        ],
        compiler_params=pltpu.CompilerParams(
            collective_id=0, has_side_effects=True, vmem_limit_bytes=44 * 1024 * 1024
        ),
    )(
        links,
        scale,
        user_emb[0],
        item_emb[0],
        weight,
        grad_user[0],
        grad_item[0],
        tile_values[0],
    )
    grad_user_emb, grad_item_emb, grad_weight = outs
    if not in_kernel:
        grad_weight = lax.psum(grad_weight, ("au", "ia"))
    return (grad_user_emb[None], grad_item_emb[None], grad_weight)


def solution(mesh):
    return jax.shard_map(
        per_device,
        mesh=mesh,
        in_specs=(
            P("au", "ia", None),
            P("ia", "au", None),
            P(),
            P("au", "ia", None),
            P("ia", "au", None),
            P("au", "ia", None, None),
            P("au", "ia"),
            P("au", "ia"),
            P("au", "ia"),
            P("au", "ia"),
        ),
        out_specs=(P("au", "ia", None), P("ia", "au", None), P()),
        check_vma=False,
    )
```

time: 432 us -> 57 us (0.13)
  waiting for transfers between devices: 228 us -> 0 us
  other arithmetic: 79 us -> 2.92 us
  Pallas kernels: 0 us -> 43.7 us
  matrix products: 36.2 us -> 0 us
  blocking collectives: 33.3 us -> 0 us
  local copies, waits for them, and re-layouts: 37.7 us -> 8.7 us
  between operations: 14.5 us -> 1.31 us
    psum x1 -> x0, waiting for transfers between devices: 125 us -> none  [per_device(): lax.psum(weight_part, ('au', 'ia')) / math.sqrt(user_count + item_count)]
    reduce_scatter x2 -> x0, waiting for transfers between devices: 103 us -> none  [the longest x1 103 us: reduce_items(): lax.psum_scatter(item_total.reshape(-1, width).astype(jnp.bfloat16), 'au'...]
    scatter-add x24 -> x0, other arithmetic: 55.1 us -> none  [the longest x12 39.2 us: one_turn(): user_total = user_total.at[row_pick].add(forward * inverse)]
    pallas_call x0 -> x1, Pallas kernels: none -> 43.7 us  [per_device(): pl.pallas_call(functools.partial(kernel, (n_au, n_ia, in_kernel, factor))...]
    dot_general x28 -> x0, matrix products: 36.2 us -> none  [the longest x12 14.9 us: one_turn(): jnp.einsum('gic,gid->gcd', values, user_source[row_pick], preferred_eleme...]
    all_gather x1 -> x0, blocking collectives: 33.3 us -> none  [fetch_items(): cotangent = lax.all_gather(grad_item, 'au', axis=1, tiled=True)]
    gather x24 -> x0, local copies, waits for them, and re-layouts: 28.8 us -> none  [the longest x12 21.8 us: one_turn(): user_source[row_pick]]
    select_n x48 -> x2, other arithmetic: 19.2 us -> 1.34 us  [the longest x1 0.68 us: per_device(): place = jnp.where(live, tile_rows[0] * item_tiles + tile_cols[0], -1)]
  transfers between devices with their start and end apart: 4 -> 0, of which waited for: 2 -> 0; matrix products, arithmetic and copies ran while one was open for 35% -> 0% of each run, Pallas kernels for 0% -> 0%
where the time goes in v1:
time: 57 us; the launch traced here: 56.7 us
  Pallas kernels  43.7 us (77%)
  local copies, waits for them, and re-layouts  8.7 us (15%)
  other arithmetic  2.92 us (5%)
  between operations  1.31 us (2%)
    pallas_call x1, Pallas kernels, per_device(): pl.pallas_call(functools.partial(kernel, (n_au, n_ia, in_kernel, factor))...  43.7 us
    unnamed x15, local copies, waits for them, and re-layouts  8.7 us

profile of v1, /device:TPU:0, one launch (start us, length us, event | category | flops | bytes accessed | tf_op | source)
XLA Modules:
  0.0 56.7 jit_solution(2490231138052542544)
XLA Ops:
  1.3 0.7 %compare_select_fusion.1.scale_ref = f32[128]{0:T(128)S(1)} fusion(s32[1,128]{1,0:T(1,128)} %param.18, s32[]{:T(128)} %bitcast.16), kind=kLoop, calls=%fused_computation.4 | loop fusion | flops 512 | bytes 1028 | tf_op jit(solution)/shard_map/jit(_where)/select_n | solution.py:429
  1.9 0.7 %compare_select_fusion.2 = s32[128]{0:T(128)S(1)} fusion(s32[]{:T(128)} %bitcast.15, s32[1,128]{1,0:T(1,128)} %param.17, s32[1,128]{1,0:T(1,128)} %param.16), kind=kLoop, calls=%fused_computation.5 | loop fusion | flops 512 | bytes 1540 | tf_op jit(solution)/shard_map/jit(_where)/select_n | solution.py:424
  2.6 0.7 %fusion.1 = s32[128]{0:T(128)S(1)} fusion(s32[]{:T(128)} %bitcast.14, s32[1,128]{1,0:T(1,128)} %param.17, s32[1,128]{1,0:T(1,128)} %param.16), kind=kLoop, calls=%fused_computation.7 | loop fusion | flops 512 | bytes 1540 | tf_op jit(solution)/shard_map/eq | solution.py:427
  3.3 0.9 %select_reduce_fusion.link_ref = s32[256]{0:T(256)S(1)} fusion(s32[128]{0:T(128)S(1)} %iota_add_fusion, s32[256]{0:T(256)} %constant.3.clone.1, s32[128]{0:T(128)S(1)} %fusion.1, s32[256]{0:T(256)S(1)} %pad_add_fusion), kind=kLoop, calls=%fused_computation | loop fusion | flops 163584 | bytes 4096 | tf_op jit(solution)/shard_map/reduce_max | solution.py:428
  4.2 0.0 copy-start
  4.2 2.2 %copy-done = bf16[1,128,128,128]{3,2,1,0:T(8,128)(2,1)S(1)} copy-done((bf16[1,128,128,128]{3,2,1,0:T(8,128)(2,1)S(1)}, bf16[1,128,128,128]{3,2,1,0:T(8,128)(2,1)}, u32[]{:S(2)}) %copy-start) | copy-done | bytes 4194328
  6.4 0.0 copy-start.1
  6.4 0.9 %copy-done.1 = bf16[1,512,256]{2,1,0:T(8,128)(2,1)S(1)} copy-done((bf16[1,512,256]{2,1,0:T(8,128)(2,1)S(1)}, bf16[1,512,256]{2,1,0:T(8,128)(2,1)}, u32[]{:S(2)}) %copy-start.1) | copy-done | bytes 262168
  7.4 0.0 copy-start.2
  7.4 0.9 %copy-done.2 = bf16[1,512,256]{2,1,0:T(8,128)(2,1)S(1)} copy-done((bf16[1,512,256]{2,1,0:T(8,128)(2,1)S(1)}, bf16[1,512,256]{2,1,0:T(8,128)(2,1)}, u32[]{:S(2)}) %copy-start.2) | copy-done | bytes 262168
  8.3 0.0 copy-start.3
  8.3 0.9 %copy-done.3 = bf16[256,256]{1,0:T(8,128)(2,1)S(1)} copy-done((bf16[256,256]{1,0:T(8,128)(2,1)S(1)}, bf16[256,256]{1,0:T(8,128)(2,1)}, u32[]{:S(2)}) %copy-start.3) | copy-done | bytes 131096
  9.2 0.0 copy-start.4
  9.2 0.8 %copy-done.4 = bf16[1,128,256]{2,1,0:T(8,128)(2,1)S(1)} copy-done((bf16[1,128,256]{2,1,0:T(8,128)(2,1)S(1)}, bf16[1,128,256]{2,1,0:T(8,128)(2,1)}, u32[]{:S(2)}) %copy-start.4) | copy-done | bytes 65560
  10.1 0.0 copy-start.5
  10.1 0.8 %copy-done.5 = bf16[1,128,256]{2,1,0:T(8,128)(2,1)S(1)} copy-done((bf16[1,128,256]{2,1,0:T(8,128)(2,1)S(1)}, bf16[1,128,256]{2,1,0:T(8,128)(2,1)}, u32[]{:S(2)}) %copy-start.5) | copy-done | bytes 65560
  10.9 43.7 %shard_map.121 = (bf16[512,256]{1,0:T(8,128)(2,1)S(1)}, bf16[128,256]{1,0:T(8,128)(2,1)S(1)}, f32[256,256]{1,0:T(8,128)S(1)}) custom-call(s32[256]{0:T(256)S(1)} %select_reduce_fusion.link_ref, f32[128]{0:T(128)S(1)} %compare_select_fusion.1.scale_ref, bf16[512,256]{1,0:T(8,128)(2,1)S(1)} %bitcast.18, bf16[128,256]{1,0:T(8,128)(2,1)S(1)} %bitcast.21, ...), custom_call_target="tpu_custom_call" | custom-call | tf_op jit(solution)/shard_map/pallas_call | solution.py:442
  54.6 0.7 %copy.17 = bf16[1,512,256]{2,1,0:T(8,128)(2,1)} copy(bf16[1,512,256]{2,1,0:T(8,128)(2,1)S(1)} %bitcast.20) | data formatting | bytes 524288
  55.3 0.6 %copy.18 = bf16[1,128,256]{2,1,0:T(8,128)(2,1)} copy(bf16[1,128,256]{2,1,0:T(8,128)(2,1)S(1)} %bitcast.23) | data formatting | bytes 131072
  56.0 0.7 %copy.19 = f32[256,256]{1,0:T(8,128)} copy(f32[256,256]{1,0:T(8,128)S(1)} %get-tuple-element.14) | data formatting | bytes 524288
  (3 shorter events, 0.0 us)
Async XLA Ops:
  4.2 2.2 %copy-start = (bf16[1,128,128,128]{3,2,1,0:T(8,128)(2,1)S(1)}, bf16[1,128,128,128]{3,2,1,0:T(8,128)(2,1)}, u32[]{:S(2)}) copy-start(bf16[1,128,128,128]{3,2,1,0:T(8,128)(2,1)} %param.15) | copy-start | bytes 12582916
  6.4 0.9 %copy-start.1 = (bf16[1,512,256]{2,1,0:T(8,128)(2,1)S(1)}, bf16[1,512,256]{2,1,0:T(8,128)(2,1)}, u32[]{:S(2)}) copy-start(bf16[1,512,256]{2,1,0:T(8,128)(2,1)} %param.10) | copy-start | bytes 786436
  7.4 0.9 %copy-start.2 = (bf16[1,512,256]{2,1,0:T(8,128)(2,1)S(1)}, bf16[1,512,256]{2,1,0:T(8,128)(2,1)}, u32[]{:S(2)}) copy-start(bf16[1,512,256]{2,1,0:T(8,128)(2,1)} %param.13) | copy-start | bytes 786436
  8.3 0.9 %copy-start.3 = (bf16[256,256]{1,0:T(8,128)(2,1)S(1)}, bf16[256,256]{1,0:T(8,128)(2,1)}, u32[]{:S(2)}) copy-start(bf16[256,256]{1,0:T(8,128)(2,1)} %weight.1) | copy-start | bytes 393220
  9.2 0.8 %copy-start.4 = (bf16[1,128,256]{2,1,0:T(8,128)(2,1)S(1)}, bf16[1,128,256]{2,1,0:T(8,128)(2,1)}, u32[]{:S(2)}) copy-start(bf16[1,128,256]{2,1,0:T(8,128)(2,1)} %param.11) | copy-start | bytes 196612
  10.1 0.8 %copy-start.5 = (bf16[1,128,256]{2,1,0:T(8,128)(2,1)S(1)}, bf16[1,128,256]{2,1,0:T(8,128)(2,1)}, u32[]{:S(2)}) copy-start(bf16[1,128,256]{2,1,0:T(8,128)(2,1)} %param.14) | copy-start | bytes 196612

commit v2 on v1

--- a/solution.py
+++ b/solution.py
@@ -89,11 +89,6 @@
             self.near(step).start()
         self.near(0).start()
 
-    def keep_own(self):
-        self.full[pl.ds(pl.multiple_of(self.ring.me * self.rows, self.rows), self.rows), :] = (
-            self.shard[...]
-        )
-
     def forward(self, step):
         self.near(step, True).wait_recv()
         self.far(step).start()
@@ -177,19 +172,44 @@
     return dot(embedded, low, ((0,), (0,))) + dot(embedded, rest, ((0,), (0,)))
 
 
+def slot_links(rows, columns, live_count, item_tiles, places):
+    cap = rows.shape[1]
+    lane = lax.broadcasted_iota(jnp.int32, (cap, cap), 1)
+    slot = lax.broadcasted_iota(jnp.int32, (cap, cap), 0)
+    place = jnp.broadcast_to(rows * item_tiles + columns, (cap, cap))
+    place = jnp.where(lane < live_count, place, -1)
+    held = place.T
+    earlier = jnp.where((held == place) & (slot < lane) & (held >= 0), slot + 1, 0)
+    links = [jnp.max(earlier, axis=0, keepdims=True)]
+    for first in range(0, places, cap):
+        latest = jnp.where(held == lane + first, slot + 1, 0)
+        links.append(jnp.max(latest, axis=0, keepdims=True))
+    return links
+
+
 def kernel(
     sizes,
-    link_ref,
-    scale_ref,
-    user_emb,
-    item_emb,
-    weight,
+    count_ref,
+    tile_rows,
+    tile_cols,
+    tile_norm,
+    user_emb_hbm,
+    item_emb_hbm,
+    weight_hbm,
     grad_user,
     grad_item,
     tiles_hbm,
     out_user,
     out_item,
     out_weight,
+    user_emb,
+    item_emb,
+    weight,
+    tables,
+    link_rows,
+    scale_row,
+    link_ref,
+    scale_ref,
     tiles,
     sums,
     adjacency,
@@ -208,6 +228,8 @@
     piece_own,
     piece_all,
     load_sem,
+    own_sem,
+    table_sem,
     ia_gather_sems,
     au_gather_sems,
     ia_reduce_sems,
@@ -231,8 +253,28 @@
         span = pl.ds(index * part, part)
         return pltpu.make_async_copy(tiles_hbm.at[span], tiles.at[span], load_sem.at[index])
 
+    table_loads = [
+        pltpu.make_async_copy(source, tables.at[index], table_sem.at[index])
+        for index, source in enumerate((tile_rows, tile_cols, tile_norm))
+    ]
+    for copy in table_loads:
+        copy.start()
     for index in range(LOAD_PARTS):
         load(index).start()
+
+    def own(full, shard, ring, index):
+        rows = shard.shape[0]
+        return pltpu.make_async_copy(shard, block_of(full, ring.me, rows), own_sem.at[index])
+
+    own_loads = [
+        own(user_full, grad_user, ia, 0),
+        own(item_full, grad_item, au, 1),
+        pltpu.make_async_copy(user_emb_hbm, user_emb, own_sem.at[2]),
+        pltpu.make_async_copy(item_emb_hbm, item_emb, own_sem.at[3]),
+        pltpu.make_async_copy(weight_hbm, weight, own_sem.at[4]),
+    ]
+    for copy in own_loads:
+        copy.start()
 
     barrier = pltpu.get_barrier_semaphore()
     if in_kernel:
@@ -263,14 +305,30 @@
     gather_item = Gather(au, grad_item, item_full, [au_gather_sems.at[i] for i in range(4)])
     gather_item.start()
     gather_user.start()
-    gather_user.keep_own()
-    gather_item.keep_own()
+
+    for copy in table_loads:
+        copy.wait()
+    places = user_tiles * item_tiles
+    live_count = count_ref[0, 0]
+    links = slot_links(tables[0], tables[1], live_count, item_tiles, places)
+    for index, row in enumerate(links):
+        link_rows[index : index + 1, :] = row
+    alive = lax.broadcasted_iota(jnp.int32, (1, cap), 1) < live_count
+    scale_row[...] = jnp.where(alive, 1.0 / tables[2].astype(jnp.float32), 0.0)
+    to_scalars = [
+        pltpu.make_async_copy(link_rows, link_ref, table_sem.at[3]),
+        pltpu.make_async_copy(scale_row, scale_ref, table_sem.at[4]),
+    ]
+    for copy in to_scalars:
+        copy.start()
+    for copy in to_scalars:
+        copy.wait()
 
     sums[0] = jnp.zeros(sums.shape[1:], jnp.float32)
 
     def add_slot(slot, carry):
         sums[slot + 1] = (
-            tiles[slot].astype(jnp.float32) * scale_ref[slot] + sums[link_ref[slot]]
+            tiles[slot].astype(jnp.float32) * scale_ref[0, slot] + sums[link_ref[0, slot]]
         )
         return carry
 
@@ -283,7 +341,8 @@
 
     def place_row(row, carry):
         for column in range(item_tiles):
-            tile = sums[link_ref[cap + row * item_tiles + column]]
+            place = row * item_tiles + column
+            tile = sums[link_ref[1 + place // cap, place % cap]]
             adjacency[
                 pl.ds(pl.multiple_of(row * edge, edge), edge), pl.ds(column * edge, edge)
             ] = tile.astype(jnp.bfloat16)
@@ -297,6 +356,8 @@
         gather_user.forward(step)
 
     wide = 2 * edge
+    for copy in own_loads:
+        copy.wait()
     gather_user.finish()
 
     def item_product(index, carry):
@@ -365,11 +426,8 @@
             )
 
         def run(action):
-            def body(step, carry):
+            for step in range(1, count):
                 action(step)
-                return carry
-
-            lax.fori_loop(1, count, body, 0)
 
         run(lambda step: scatter(step).start())
         out_item[...] = dot(item_low, weight[...], ((1,), (1,))).astype(jnp.bfloat16)
@@ -419,15 +477,7 @@
     item_tiles = items // edge
     places = (users // edge) * item_tiles
 
-    slots = jnp.arange(cap, dtype=jnp.int32)
-    live = slots < tile_count[0, 0]
-    place = jnp.where(live, tile_rows[0] * item_tiles + tile_cols[0], -1)
-    wanted = jnp.concatenate([place, jnp.arange(places, dtype=jnp.int32)])
-    limit = jnp.concatenate([slots, jnp.full((places,), cap, jnp.int32)])
-    match = (place[None] == wanted[:, None]) & (slots[None] < limit[:, None])
-    links = jnp.max(jnp.where(match, slots[None] + 1, 0), axis=1)
-    scale = jnp.where(live, 1.0 / tile_norm[0].astype(jnp.float32), 0.0)
-
+    link_rows = 1 + -(-places // cap)
     piece_rows = width * (width // LANES) // count
     in_kernel = piece_rows % 16 == 0 and piece_rows > 0 and width % piece_rows == 0
     pieces = count if in_kernel else 1
@@ -446,9 +496,17 @@
             jax.ShapeDtypeStruct((item_rows, width), bf16),
             jax.ShapeDtypeStruct((width, width), f32),
         ),
-        in_specs=[smem, smem, vmem, vmem, vmem, vmem, vmem, pl.BlockSpec(memory_space=pl.ANY)],
+        in_specs=[smem] + [pl.BlockSpec(memory_space=pltpu.HBM)] * 9,
         out_specs=(vmem, vmem, vmem),
         scratch_shapes=[
+            pltpu.VMEM((user_rows, width), bf16),
+            pltpu.VMEM((item_rows, width), bf16),
+            pltpu.VMEM((width, width), bf16),
+            pltpu.VMEM((3, 1, cap), jnp.int32),
+            pltpu.VMEM((link_rows, cap), jnp.int32),
+            pltpu.VMEM((1, cap), f32),
+            pltpu.SMEM((link_rows, cap), jnp.int32),
+            pltpu.SMEM((1, cap), f32),
             pltpu.VMEM((cap, edge, edge), bf16),
             pltpu.VMEM((cap + 1, edge, edge), f32),
             pltpu.VMEM((users, items), bf16),
@@ -467,6 +525,8 @@
             pltpu.VMEM((piece_rows, LANES), bf16),
             pltpu.VMEM((pieces, piece_rows, LANES), bf16),
             dma((LOAD_PARTS,)),
+            dma((5,)),
+            dma((5,)),
             dma((4, half_ia)),
             dma((4, half_au)),
             dma((4, half_ia)),
@@ -474,11 +534,13 @@
             dma((4, pieces)),
         ],
         compiler_params=pltpu.CompilerParams(
-            collective_id=0, has_side_effects=True, vmem_limit_bytes=44 * 1024 * 1024
+            collective_id=0, has_side_effects=True, vmem_limit_bytes=62 * 1024 * 1024
         ),
     )(
-        links,
-        scale,
+        tile_count,
+        tile_rows,
+        tile_cols,
+        tile_norm,
         user_emb[0],
         item_emb[0],
         weight,

time: 57 us -> 49.4 us (0.87)
  local copies, waits for them, and re-layouts: 8.7 us -> 4.81 us
  other arithmetic: 2.92 us -> 0 us
  Pallas kernels: 43.7 us -> 43.1 us
    unnamed x15 -> x3, local copies, waits for them, and re-layouts: 8.7 us -> 4.81 us
    select_n x2 -> x0, other arithmetic: 1.34 us -> none  [the longest x1 0.68 us: per_device(): place = jnp.where(live, tile_rows[0] * item_tiles + tile_cols[0], -1)]
    reduce_max x1 -> x0, other arithmetic: 0.89 us -> none  [per_device(): links = jnp.max(jnp.where(match, slots[None] + 1, 0), axis=1)]
    eq x1 -> x0, other arithmetic: 0.68 us -> none  [per_device(): match = (place[None] == wanted[:, None]) & (slots[None] < limit[:, None])]
    pallas_call x1, Pallas kernels: 43.7 us -> 43.1 us  [per_device(): pl.pallas_call(functools.partial(kernel, (n_au, n_ia, in_kernel, factor))...]
where the time goes in v2:
time: 49.4 us; the launch traced here: 49.2 us
  Pallas kernels  43.1 us (87%)
  local copies, waits for them, and re-layouts  4.81 us (10%)
  between operations  1.29 us (3%)
    pallas_call x1, Pallas kernels, per_device(): pl.pallas_call(functools.partial(kernel, (n_au, n_ia, in_kernel, factor))...  43.1 us
    unnamed x3, local copies, waits for them, and re-layouts  4.81 us

profile of v2, /device:TPU:0, one launch (start us, length us, event | category | flops | bytes accessed | tf_op | source)
XLA Modules:
  0.0 49.2 jit_solution(578477480625337839)
XLA Ops:
  1.3 43.1 %shard_map.121 = (bf16[512,256]{1,0:T(8,128)(2,1)}, bf16[128,256]{1,0:T(8,128)(2,1)}, f32[256,256]{1,0:T(8,128)}) custom-call(s32[1,1]{1,0:T(1,128)S(6)} %copy.16.count_ref, s32[1,128]{1,0:T(1,128)} %tile_rows.1, s32[1,128]{1,0:T(1,128)} %tile_cols.1, s32[1,128]{1,0:T(1,128)} %tile_norm.1, bf16[512,256]{1,0:T(8,128)(2,1)} %bitcast.8, ...), custom_call_target="tpu_custom_call" | custom-call | tf_op jit(solution)/shard_map/pallas_call | solution.py:492
  44.4 1.7 %copy.17 = bf16[1,512,256]{2,1,0:T(8,128)(2,1)} copy(bf16[1,512,256]{2,1,0:T(8,128)(2,1)} %bitcast.10) | data formatting | bytes 524288
  46.0 1.5 %copy.18 = bf16[1,128,256]{2,1,0:T(8,128)(2,1)} copy(bf16[1,128,256]{2,1,0:T(8,128)(2,1)} %bitcast.13) | data formatting | bytes 131072
  47.5 1.7 %copy.19 = f32[256,256]{1,0:T(8,128)} copy(f32[256,256]{1,0:T(8,128)} %get-tuple-element.14) | data formatting | bytes 524288

commit v3 on v2

--- a/solution.py
+++ b/solution.py
@@ -199,9 +199,11 @@
     grad_user,
     grad_item,
     tiles_hbm,
+    out_user_hbm,
+    out_item_hbm,
+    out_weight,
     out_user,
     out_item,
-    out_weight,
     user_emb,
     item_emb,
     weight,
@@ -277,29 +279,11 @@
         copy.start()
 
     barrier = pltpu.get_barrier_semaphore()
-    if in_kernel:
-
-        def greet(step, carry):
-            pl.semaphore_signal(
-                barrier, inc=1, device_id=peer((me + step) % count), device_id_type=MESH
-            )
-            return carry
-
-        lax.fori_loop(1, count, greet, 0)
-        pl.semaphore_wait(barrier, count - 1)
-    else:
-        for ring in (au, ia):
-            pl.semaphore_signal(
-                barrier, inc=1, device_id=ring.at(ring.other(ring.pair)), device_id_type=MESH
-            )
-            for step in range(1, ring.half):
-                pl.semaphore_signal(
-                    barrier,
-                    inc=1,
-                    device_id=ring.at(ring.same(ring.ahead(step))),
-                    device_id_type=MESH,
-                )
-        pl.semaphore_wait(barrier, au.half + ia.half)
+    for ring in (au, ia):
+        for step in range(ring.half):
+            index = ring.same(ring.ahead(step)) if step else ring.other(ring.pair)
+            pl.semaphore_signal(barrier, inc=1, device_id=ring.at(index), device_id_type=MESH)
+    pl.semaphore_wait(barrier, au.half + ia.half)
 
     gather_user = Gather(ia, grad_user, user_full, [ia_gather_sems.at[i] for i in range(4)])
     gather_item = Gather(au, grad_item, item_full, [au_gather_sems.at[i] for i in range(4)])
@@ -391,6 +375,9 @@
     q_user = reduce_user.finish()
     user_low = q_user.astype(jnp.bfloat16)
     out_user[...] = dot(user_low, weight[...], ((1,), (1,))).astype(jnp.bfloat16)
+    keep_user = pltpu.make_async_copy(out_user, out_user_hbm, own_sem.at[5])
+    keep_item = pltpu.make_async_copy(out_item, out_item_hbm, own_sem.at[6])
+    keep_user.start()
     term = embedded_product(user_emb[...], q_user, user_low)
     q_item = reduce_item.finish()
     item_low = q_item.astype(jnp.bfloat16)
@@ -431,6 +418,7 @@
 
         run(lambda step: scatter(step).start())
         out_item[...] = dot(item_low, weight[...], ((1,), (1,))).astype(jnp.bfloat16)
+        keep_item.start()
         run(lambda step: scatter(step).wait_recv())
         total = piece_out[me].astype(jnp.float32)
         for step in range(1, count):
@@ -448,8 +436,11 @@
         run(lambda step: spread(step).wait_send())
     else:
         out_item[...] = dot(item_low, weight[...], ((1,), (1,))).astype(jnp.bfloat16)
+        keep_item.start()
         out_weight[...] = term * factor
 
+    keep_user.wait()
+    keep_item.wait()
     gather_user.drain()
     gather_item.drain()
     reduce_user.drain()
@@ -486,6 +477,7 @@
     half_au, half_ia = n_au // 2, n_ia // 2
     bf16, f32 = jnp.bfloat16, jnp.float32
     vmem = pl.BlockSpec(memory_space=pltpu.VMEM)
+    hbm = pl.BlockSpec(memory_space=pltpu.HBM)
     smem = pl.BlockSpec(memory_space=pltpu.SMEM)
     dma = pltpu.SemaphoreType.DMA
 
@@ -496,9 +488,11 @@
             jax.ShapeDtypeStruct((item_rows, width), bf16),
             jax.ShapeDtypeStruct((width, width), f32),
         ),
-        in_specs=[smem] + [pl.BlockSpec(memory_space=pltpu.HBM)] * 9,
-        out_specs=(vmem, vmem, vmem),
+        in_specs=[smem] + [hbm] * 9,
+        out_specs=(hbm, hbm, vmem),
         scratch_shapes=[
+            pltpu.VMEM((user_rows, width), bf16),
+            pltpu.VMEM((item_rows, width), bf16),
             pltpu.VMEM((user_rows, width), bf16),
             pltpu.VMEM((item_rows, width), bf16),
             pltpu.VMEM((width, width), bf16),
@@ -525,7 +519,7 @@
             pltpu.VMEM((piece_rows, LANES), bf16),
             pltpu.VMEM((pieces, piece_rows, LANES), bf16),
             dma((LOAD_PARTS,)),
-            dma((5,)),
+            dma((7,)),
             dma((5,)),
             dma((4, half_ia)),
             dma((4, half_au)),

time: 49.4 us -> 47.5 us (0.962)
  Pallas kernels: 43.1 us -> 41.2 us
    pallas_call x1, Pallas kernels: 43.1 us -> 41.2 us  [per_device(): pl.pallas_call(functools.partial(kernel, (n_au, n_ia, in_kernel, factor))...]
where the time goes in v3:
time: 47.5 us; the launch traced here: 47.3 us
  Pallas kernels  41.2 us (87%)
  local copies, waits for them, and re-layouts  4.81 us (10%)
  between operations  1.29 us (3%)
    pallas_call x1, Pallas kernels, per_device(): pl.pallas_call(functools.partial(kernel, (n_au, n_ia, in_kernel, factor))...  41.2 us
    unnamed x3, local copies, waits for them, and re-layouts  4.81 us

profile of v3, /device:TPU:0, one launch (start us, length us, event | category | flops | bytes accessed | tf_op | source)
XLA Modules:
  0.0 47.3 jit_solution(11076512690090267136)
XLA Ops:
  1.3 41.2 %shard_map.121 = (bf16[512,256]{1,0:T(8,128)(2,1)}, bf16[128,256]{1,0:T(8,128)(2,1)}, f32[256,256]{1,0:T(8,128)}) custom-call(s32[1,1]{1,0:T(1,128)S(6)} %copy.16.count_ref, s32[1,128]{1,0:T(1,128)} %tile_rows.1, s32[1,128]{1,0:T(1,128)} %tile_cols.1, s32[1,128]{1,0:T(1,128)} %tile_norm.1, bf16[512,256]{1,0:T(8,128)(2,1)} %bitcast.8, ...), custom_call_target="tpu_custom_call" | custom-call | tf_op jit(solution)/shard_map/pallas_call | solution.py:484
  42.4 1.7 %copy.17 = bf16[1,512,256]{2,1,0:T(8,128)(2,1)} copy(bf16[1,512,256]{2,1,0:T(8,128)(2,1)} %bitcast.10) | data formatting | bytes 524288
  44.1 1.5 %copy.18 = bf16[1,128,256]{2,1,0:T(8,128)(2,1)} copy(bf16[1,128,256]{2,1,0:T(8,128)(2,1)} %bitcast.13) | data formatting | bytes 131072
  45.6 1.7 %copy.19 = f32[256,256]{1,0:T(8,128)} copy(f32[256,256]{1,0:T(8,128)} %get-tuple-element.14) | data formatting | bytes 524288

commit v4 on v3

--- a/solution.py
+++ b/solution.py
@@ -445,6 +445,19 @@
     gather_item.drain()
     reduce_user.drain()
     reduce_item.drain()
+
+
+def hand_on(*refs):
+    sems = refs[-1]
+    half = (len(refs) - 1) // 2
+    copies = [
+        pltpu.make_async_copy(refs[index], refs[half + index], sems.at[index])
+        for index in range(half)
+    ]
+    for copy in copies:
+        copy.start()
+    for copy in copies:
+        copy.wait()
 
 
 def per_device(
@@ -542,7 +555,14 @@
         grad_item[0],
         tile_values[0],
     )
-    grad_user_emb, grad_item_emb, grad_weight = outs
+    grad_user_emb, grad_item_emb, grad_weight = pl.pallas_call(
+        hand_on,
+        out_shape=tuple(jax.ShapeDtypeStruct(out.shape, out.dtype) for out in outs),
+        in_specs=[hbm] * len(outs),
+        out_specs=(hbm,) * len(outs),
+        scratch_shapes=[dma((len(outs),))],
+        compiler_params=pltpu.CompilerParams(vmem_limit_bytes=62 * 1024 * 1024),
+    )(*outs)
     if not in_kernel:
         grad_weight = lax.psum(grad_weight, ("au", "ia"))
     return (grad_user_emb[None], grad_item_emb[None], grad_weight)

time: 47.5 us -> 61.6 us (1.30)
  Pallas kernels: 41.2 us -> 60.2 us
  local copies, waits for them, and re-layouts: 4.81 us -> 0 us
    pallas_call x0 -> x1, Pallas kernels: none -> 19 us  [per_device(): pl.pallas_call(hand_on, out_shape=tuple((jax.ShapeDtypeStruct(out.shape,...]
    unnamed x3 -> x0, local copies, waits for them, and re-layouts: 4.81 us -> none
where the time goes in v4:
time: 61.6 us; the launch traced here: 61.5 us
  Pallas kernels  60.2 us (98%)
  between operations  1.29 us (2%)
    pallas_call x1, Pallas kernels, per_device(): pl.pallas_call(functools.partial(kernel, (n_au, n_ia, in_kernel, factor))...  41.2 us
    pallas_call x1, Pallas kernels, per_device(): pl.pallas_call(hand_on, out_shape=tuple((jax.ShapeDtypeStruct(out.shape,...  19 us

profile of v4, /device:TPU:0, one launch (start us, length us, event | category | flops | bytes accessed | tf_op | source)
XLA Modules:
  0.0 61.5 jit_solution(2306124448163905128)
XLA Ops:
  1.3 41.2 %shard_map.121 = (bf16[512,256]{1,0:T(8,128)(2,1)}, bf16[128,256]{1,0:T(8,128)(2,1)}, f32[256,256]{1,0:T(8,128)}) custom-call(s32[1,1]{1,0:T(1,128)S(6)} %copy.13.count_ref, s32[1,128]{1,0:T(1,128)} %tile_rows.1, s32[1,128]{1,0:T(1,128)} %tile_cols.1, s32[1,128]{1,0:T(1,128)} %tile_norm.1, bf16[512,256]{1,0:T(8,128)(2,1)} %bitcast.8, ...), custom_call_target="tpu_custom_call" | custom-call | tf_op jit(solution)/shard_map/pallas_call | solution.py:497
  42.5 19.0 %shard_map.122 = (bf16[512,256]{1,0:T(8,128)(2,1)}, bf16[128,256]{1,0:T(8,128)(2,1)}, f32[256,256]{1,0:T(8,128)}) custom-call(bf16[512,256]{1,0:T(8,128)(2,1)} %get-tuple-element.9.refs_0_, bf16[128,256]{1,0:T(8,128)(2,1)} %get-tuple-element.10.refs_1_, f32[256,256]{1,0:T(8,128)} %get-tuple-element.11.refs_2_), custom_call_target="tpu_custom_call" | custom-call | tf_op jit(solution)/shard_map/pallas_call | solution.py:558
